TPU v7x, 32 devices: a whole 2x2x4 slice. The times are simulated.
32 devices in a mesh: groups: 2 (over y), span: 16 (over z, x, core).
Axes of the slice: x: 2, y: 2, z: 4, core: 2. Of those that a mesh axis runs over, the one named last changes fastest.
Arguments:
- queries: bfloat16 [8192, 3072], P(('groups', 'span')), parts along dimension 0, may hold values from -48 to 48
- keys: bfloat16 [8192, 1024], P(('groups', 'span')), parts along dimension 0, may hold values from -8 to 8
- values: bfloat16 [8192, 1024], P(('groups', 'span')), parts along dimension 0, may hold values from -6 to 6
- lookback: int32 [32], P(('groups', 'span')), parts along dimension 0, may hold values from 0 to 4, as said below
- w_out: bfloat16 [3072, 256], replicated, may hold values from -0.109375 to 0.109375
- conv_first: bfloat16 [3, 3, 3, 256, 256], replicated, may hold values from -0.078125 to 0.078125
- conv_second: bfloat16 [3, 3, 3, 256, 256], replicated, may hold values from -0.078125 to 0.078125
Outputs:
- decoded: bfloat16 [8192, 256], P(('groups', 'span')), parts along dimension 0
There are 2 independent parts, one for each index of `groups`. A program takes and returns all parts, laid end to end along the dimension named above; an argument that names none is the same for every part. Nothing has to cross between parts.
Inputs may be any that keep to these rules, and one draw needn't show every extreme that they name: lookback[c] is at most c; the value 4 is reached in every draw.
All inputs are finite; a program needn't handle non-finite values.
Results may differ from a plain program's by a relative error of at most 0.007.
Values may be sent and summed in bfloat16 or wider, within the bound.
A program may use at most 64 MiB of HBM per device.

v0:
```python
import jax
import jax.numpy as jnp
from jax import lax
from jax.sharding import PartitionSpec as P

HEAD_DIM = 128
FRAMES = 4
ROWS = 8
COLS = 8


def passed_along(block, axis, distance):
    devices = range(lax.axis_size(axis))
    route = [(i - distance, i) for i in devices if i - distance in devices]
    return lax.ppermute(block, axis, route)


def attend(query_rows, key_rows, value_rows, visible):
    tok = query_rows.shape[0]
    groups = key_rows.shape[1] // HEAD_DIM
    ratio = query_rows.shape[1] // key_rows.shape[1]
    scale = 1.0 / jnp.sqrt(jnp.float32(HEAD_DIM))
    grouped = query_rows.reshape(tok, groups, ratio, HEAD_DIM)
    pieces = []
    for group in range(groups):
        qpart = grouped[:, group]
        kpart = key_rows[:, group * HEAD_DIM : (group + 1) * HEAD_DIM]
        vpart = value_rows[:, group * HEAD_DIM : (group + 1) * HEAD_DIM]
        scores = jnp.einsum("trd,sd->rts", qpart, kpart, preferred_element_type=jnp.float32) * scale
        scores = jnp.where(visible[None, None, :], scores, -1e30)
        peak = jnp.max(scores, axis=-1, keepdims=True)
        weights = jnp.exp(scores - peak)
        total = jnp.sum(weights, axis=-1)
        probs = weights.astype(jnp.bfloat16)
        mixed = (
            jnp.einsum("rts,sd->rtd", probs, vpart, preferred_element_type=jnp.float32)
            / total[:, :, None]
        )
        pieces.append(jnp.transpose(mixed, (1, 0, 2)).reshape(tok, ratio * HEAD_DIM))
    return jnp.concatenate(pieces, axis=-1).astype(jnp.bfloat16)


def conv_valid(extended, weight):
    frames_out = extended.shape[0] - 2
    rows = extended.shape[1]
    cols = extended.shape[2]
    chans = extended.shape[3]
    padded = jnp.pad(extended, ((0, 0), (1, 1), (1, 1), (0, 0)))
    columns = jnp.concatenate(
        [
            padded[a : a + frames_out, b : b + rows, e : e + cols]
            for a in range(3)
            for b in range(3)
            for e in range(3)
        ],
        axis=-1,
    )
    columns = columns.reshape(frames_out * rows * cols, 27 * chans)
    return jnp.dot(
        columns, weight.reshape(27 * chans, weight.shape[4]), preferred_element_type=jnp.float32
    )


def on_device(queries, keys, values, lookback, w_out, conv_first, conv_second):
    tok = queries.shape[0]
    chans = w_out.shape[1]
    earlier = []
    current = (keys, values)
    passed = []
    for step in range(4):
        current = passed_along((current[0], current[1]), "span", 1)
        passed.append(current)
    earlier = passed[::-1]
    key_rows = jnp.concatenate([pair[0] for pair in earlier] + [keys], axis=0)
    value_rows = jnp.concatenate([pair[1] for pair in earlier] + [values], axis=0)
    block = jnp.arange(5 * tok) // tok
    visible = 4 - block <= lookback[0]
    attended = attend(queries, key_rows, value_rows, visible)
    latent = jnp.dot(attended, w_out, preferred_element_type=jnp.float32).astype(jnp.bfloat16)
    latent = latent.reshape(FRAMES, ROWS, COLS, chans)
    before = passed_along(latent[FRAMES - 2 :], "span", 1)
    hidden = jax.nn.silu(conv_valid(jnp.concatenate([before, latent], axis=0), conv_first)).astype(
        jnp.bfloat16
    )
    hidden = hidden.reshape(FRAMES, ROWS, COLS, chans)
    hidden_before = passed_along(hidden[FRAMES - 2 :], "span", 1)
    decoded = conv_valid(jnp.concatenate([hidden_before, hidden], axis=0), conv_second)
    return decoded.astype(jnp.bfloat16)


def solution(mesh):
    placed = (
        P(("groups", "span"), None),
        P(("groups", "span"), None),
        P(("groups", "span"), None),
        P(("groups", "span")),
        P(),
        P(),
        P(),
    )
    return jax.shard_map(
        on_device,
        mesh=mesh,
        in_specs=placed,
        out_specs=P(("groups", "span"), None),
        check_vma=False,
    )
```

profile of v0, /device:TPU:12, one launch (start us, length us, event | category | flops | bytes accessed | tf_op | source)
XLA Modules:
  0.0 91.2 jit_solution(8350971382979047561)
XLA Ops:
  0.0 2.2 %collective-permute-start = (bf16[256,1024]{1,0:T(8,128)(2,1)}, bf16[256,1024]{1,0:T(8,128)(2,1)}, u32[]{:S(2)}, u32[]{:S(2)}) collective-permute-start(bf16[256,1024]{1,0:T(8,128)(2,1)} %param.8), channel_id=1, source_target_pairs={{0,1},{1,2},{2,3},{3,4},{4,5},{5,6},{6,7},{7,8},{8,9},{9,10},{10,1... | collective-permute-start | bytes 1572872 | tf_op jit(solution)/shard_map/ppermute | solution.py:15
  2.2 2.1 %copy.20 = bf16[256,1024]{0,1:T(8,128)(2,1)} copy(bf16[256,1024]{1,0:T(8,128)(2,1)} %param.9) | data formatting | bytes 1048576 | tf_op args[2]
  4.2 3.5 %collective-permute-start.4 = (bf16[256,1024]{0,1:T(8,128)(2,1)}, bf16[256,1024]{0,1:T(8,128)(2,1)S(1)}, u32[]{:S(2)}, u32[]{:S(2)}) collective-permute-start(bf16[256,1024]{0,1:T(8,128)(2,1)} %copy.20), channel_id=1, source_target_pairs={{0,1},{1,2},{2,3},{3,4},{4,5},{5,6},{6,7},{7,8},{8,9},{9,10},{10,1... | collective-permute-start | bytes 1572872 | tf_op jit(solution)/shard_map/ppermute | solution.py:15
  7.7 4.2 %collective-permute-done = bf16[256,1024]{1,0:T(8,128)(2,1)} collective-permute-done((bf16[256,1024]{1,0:T(8,128)(2,1)}, bf16[256,1024]{1,0:T(8,128)(2,1)}, u32[]{:S(2)}, u32[]{:S(2)}) %collective-permute-start) | collective-permute-done | bytes 524320 | tf_op jit(solution)/shard_map/ppermute | solution.py:15
  12.0 1.9 %collective-permute-start.1 = (bf16[256,1024]{1,0:T(8,128)(2,1)}, bf16[256,1024]{1,0:T(8,128)(2,1)S(1)}, u32[]{:S(2)}, u32[]{:S(2)}) collective-permute-start(bf16[256,1024]{1,0:T(8,128)(2,1)} %collective-permute-done), channel_id=1, source_target_pairs={{0,1},{1,2},{2,3},{3,4},{4,5},{5,6},{6,7},{7,8},{8,9},{9,10},{10,1... | collective-permute-start | bytes 1572872 | tf_op jit(solution)/shard_map/ppermute | solution.py:15
  13.9 3.6 %collective-permute-done.4 = bf16[256,1024]{0,1:T(8,128)(2,1)S(1)} collective-permute-done((bf16[256,1024]{0,1:T(8,128)(2,1)}, bf16[256,1024]{0,1:T(8,128)(2,1)S(1)}, u32[]{:S(2)}, u32[]{:S(2)}) %collective-permute-start.4) | collective-permute-done | bytes 524320 | tf_op jit(solution)/shard_map/ppermute | solution.py:15
  18.3 1.9 %collective-permute-start.5 = (bf16[256,1024]{0,1:T(8,128)(2,1)S(1)}, bf16[256,1024]{0,1:T(8,128)(2,1)}, u32[]{:S(2)}, u32[]{:S(2)}) collective-permute-start(bf16[256,1024]{0,1:T(8,128)(2,1)S(1)} %collective-permute-done.4), channel_id=1, source_target_pairs={{0,1},{1,2},{2,3},{3,4},{4,5},{5,6},{6,7},{7,8},{8,9},{9,10},{10,1... | collective-permute-start | bytes 1572872 | tf_op jit(solution)/shard_map/ppermute | solution.py:15
  20.2 3.4 %collective-permute-done.1 = bf16[256,1024]{1,0:T(8,128)(2,1)S(1)} collective-permute-done((bf16[256,1024]{1,0:T(8,128)(2,1)}, bf16[256,1024]{1,0:T(8,128)(2,1)S(1)}, u32[]{:S(2)}, u32[]{:S(2)}) %collective-permute-start.1) | collective-permute-done | bytes 524320 | tf_op jit(solution)/shard_map/ppermute | solution.py:15
  23.6 1.9 %collective-permute-start.2 = (bf16[256,1024]{1,0:T(8,128)(2,1)S(1)}, bf16[256,1024]{1,0:T(8,128)(2,1)}, u32[]{:S(2)}, u32[]{:S(2)}) collective-permute-start(bf16[256,1024]{1,0:T(8,128)(2,1)S(1)} %collective-permute-done.1), channel_id=1, source_target_pairs={{0,1},{1,2},{2,3},{3,4},{4,5},{5,6},{6,7},{7,8},{8,9},{9,10},{10,1... | collective-permute-start | bytes 1572872 | tf_op jit(solution)/shard_map/ppermute | solution.py:15
  25.5 4.3 %collective-permute-done.5 = bf16[256,1024]{0,1:T(8,128)(2,1)} collective-permute-done((bf16[256,1024]{0,1:T(8,128)(2,1)S(1)}, bf16[256,1024]{0,1:T(8,128)(2,1)}, u32[]{:S(2)}, u32[]{:S(2)}) %collective-permute-start.5) | collective-permute-done | bytes 524320 | tf_op jit(solution)/shard_map/ppermute | solution.py:15
  29.8 1.9 %collective-permute-start.6 = (bf16[256,1024]{0,1:T(8,128)(2,1)}, bf16[256,1024]{0,1:T(8,128)(2,1)}, u32[]{:S(2)}, u32[]{:S(2)}) collective-permute-start(bf16[256,1024]{0,1:T(8,128)(2,1)} %collective-permute-done.5), channel_id=1, source_target_pairs={{0,1},{1,2},{2,3},{3,4},{4,5},{5,6},{6,7},{7,8},{8,9},{9,10},{10,1... | collective-permute-start | bytes 1572872 | tf_op jit(solution)/shard_map/ppermute | solution.py:15
  31.7 3.7 %collective-permute-done.2 = bf16[256,1024]{1,0:T(8,128)(2,1)} collective-permute-done((bf16[256,1024]{1,0:T(8,128)(2,1)S(1)}, bf16[256,1024]{1,0:T(8,128)(2,1)}, u32[]{:S(2)}, u32[]{:S(2)}) %collective-permute-start.2) | collective-permute-done | bytes 524320 | tf_op jit(solution)/shard_map/ppermute | solution.py:15
  35.4 1.9 %collective-permute-start.3 = (bf16[256,1024]{1,0:T(8,128)(2,1)}, bf16[256,1024]{1,0:T(8,128)(2,1)}, u32[]{:S(2)}, u32[]{:S(2)}) collective-permute-start(bf16[256,1024]{1,0:T(8,128)(2,1)} %collective-permute-done.2), channel_id=1, source_target_pairs={{0,1},{1,2},{2,3},{3,4},{4,5},{5,6},{6,7},{7,8},{8,9},{9,10},{10,1... | collective-permute-start | bytes 1572872 | tf_op jit(solution)/shard_map/ppermute | solution.py:15
  37.3 2.6 %copy.18 = bf16[256,3072]{0,1:T(8,128)(2,1)} copy(bf16[256,3072]{1,0:T(8,128)(2,1)} %param.7) | data formatting | bytes 3145728 | tf_op args[0]
  41.5 1.9 %collective-permute-start.7 = (bf16[256,1024]{0,1:T(8,128)(2,1)}, bf16[256,1024]{0,1:T(8,128)(2,1)S(1)}, u32[]{:S(2)}, u32[]{:S(2)}) collective-permute-start(bf16[256,1024]{0,1:T(8,128)(2,1)} %collective-permute-done.6), channel_id=1, source_target_pairs={{0,1},{1,2},{2,3},{3,4},{4,5},{5,6},{6,7},{7,8},{8,9},{9,10},{10,1... | collective-permute-start | bytes 1572872 | tf_op jit(solution)/shard_map/ppermute | solution.py:15
  43.4 3.7 %collective-permute-done.3 = bf16[256,1024]{1,0:T(8,128)(2,1)} collective-permute-done((bf16[256,1024]{1,0:T(8,128)(2,1)}, bf16[256,1024]{1,0:T(8,128)(2,1)}, u32[]{:S(2)}, u32[]{:S(2)}) %collective-permute-start.3) | collective-permute-done | bytes 524320 | tf_op jit(solution)/shard_map/ppermute | solution.py:15
  48.2 1.1 %constant_dynamic-update-slice_fusion.8 = bf16[1280,1024]{1,0:T(8,128)(2,1)S(1)} fusion(bf16[1280,1024]{1,0:T(8,128)(2,1)S(1)} %constant_dynamic-update-slice_fusion.9, bf16[256,1024]{1,0:T(8,128)(2,1)} %collective-permute-done.2), kind=kLoop, calls=%fused_computation.189 | loop fusion | bytes 1048576
  71.9 1.9 %collective-permute-start.8 = (bf16[2,8,8,256]{3,2,1,0:T(8,128)(2,1)S(1)}, bf16[2,8,8,256]{3,2,1,0:T(8,128)(2,1)S(1)}, u32[]{:S(2)}, u32[]{:S(2)}) collective-permute-start(bf16[2,8,8,256]{3,2,1,0:T(8,128)(2,1)S(1)} %bitcast.444), channel_id=1, source_target_pairs={{0,1},{1,2},{2,3},{3,4},{4,5},{5,6},{6,7},{7,8},{8,9},{9,10},{10,1... | collective-permute-start | bytes 196616 | tf_op jit(solution)/shard_map/ppermute | solution.py:15
  73.8 4.6 %collective-permute-done.8 = bf16[2,8,8,256]{3,2,1,0:T(8,128)(2,1)S(1)} collective-permute-done((bf16[2,8,8,256]{3,2,1,0:T(8,128)(2,1)S(1)}, bf16[2,8,8,256]{3,2,1,0:T(8,128)(2,1)S(1)}, u32[]{:S(2)}, u32[]{:S(2)}) %collective-permute-start.8) | collective-permute-done | bytes 65568 | tf_op jit(solution)/shard_map/ppermute | solution.py:15
  79.4 1.1 %multiply_convert_fusion = bf16[256,256]{1,0:T(8,128)(2,1)S(1)} fusion(bf16[256,6912]{1,0:T(8,128)(2,1)S(1)} %constant_dynamic-update-slice_fusion.18, bf16[6912,256]{1,0:T(8,128)(2,1)S(1)} %bitcast.371), kind=kOutput, calls=%fused_computation.168 | convolution fusion | flops 906297344 | bytes 7208960 | tf_op jit(solution)/shard_map/dot_general | solution.py:59
  80.5 1.9 %collective-permute-start.9 = (bf16[2,8,8,256]{3,2,1,0:T(8,128)(2,1)S(1)}, bf16[2,8,8,256]{3,2,1,0:T(8,128)(2,1)S(1)}, u32[]{:S(2)}, u32[]{:S(2)}) collective-permute-start(bf16[2,8,8,256]{3,2,1,0:T(8,128)(2,1)S(1)} %bitcast.445), channel_id=1, source_target_pairs={{0,1},{1,2},{2,3},{3,4},{4,5},{5,6},{6,7},{7,8},{8,9},{9,10},{10,1... | collective-permute-start | bytes 196616 | tf_op jit(solution)/shard_map/ppermute | solution.py:15
  82.4 4.6 %collective-permute-done.9 = bf16[2,8,8,256]{3,2,1,0:T(8,128)(2,1)S(1)} collective-permute-done((bf16[2,8,8,256]{3,2,1,0:T(8,128)(2,1)S(1)}, bf16[2,8,8,256]{3,2,1,0:T(8,128)(2,1)S(1)}, u32[]{:S(2)}, u32[]{:S(2)}) %collective-permute-start.9) | collective-permute-done | bytes 65568 | tf_op jit(solution)/shard_map/ppermute | solution.py:15
  88.0 1.5 %copy-done.7 = bf16[3,3,3,256,256]{4,3,2,1,0:T(8,128)(2,1)S(1)} copy-done((bf16[3,3,3,256,256]{4,3,2,1,0:T(8,128)(2,1)S(1)}, bf16[3,3,3,256,256]{4,3,2,1,0:T(8,128)(2,1)}, u32[]{:S(2)}) %copy-start.7) | copy-done | bytes 3538968
  89.5 1.7 %convolution_convert_fusion = bf16[256,256]{1,0:T(8,128)(2,1)} fusion(bf16[256,6912]{1,0:T(8,128)(2,1)S(1)} %constant_dynamic-update-slice_fusion.45, bf16[6912,256]{1,0:T(8,128)(2,1)S(1)} %bitcast.454), kind=kOutput, calls=%fused_computation.144 | convolution fusion | flops 906035200 | bytes 7208960 | tf_op jit(solution)/shard_map/dot_general | solution.py:59
  (126 shorter events, 26.5 us)
Async XLA Ops:
  0.0 79.4 %copy-start = (bf16[3,3,3,256,256]{4,3,2,1,0:T(8,128)(2,1)S(1)}, bf16[3,3,3,256,256]{4,3,2,1,0:T(8,128)(2,1)}, u32[]{:S(2)}) copy-start(bf16[3,3,3,256,256]{4,3,2,1,0:T(8,128)(2,1)} %param.12) | copy-start | bytes 10616836
  0.0 12.0 %collective-permute-start = (bf16[256,1024]{1,0:T(8,128)(2,1)}, bf16[256,1024]{1,0:T(8,128)(2,1)}, u32[]{:S(2)}, u32[]{:S(2)}) collective-permute-start(bf16[256,1024]{1,0:T(8,128)(2,1)} %param.8), channel_id=1, source_target_pairs={{0,1},{1,2},{2,3},{3,4},{4,5},{5,6},{6,7},{7,8},{8,9},{9,10},{10,1... | collective-permute-start | bytes 1572872 | tf_op jit(solution)/shard_map/ppermute | solution.py:15
  4.2 13.2 %collective-permute-start.4 = (bf16[256,1024]{0,1:T(8,128)(2,1)}, bf16[256,1024]{0,1:T(8,128)(2,1)S(1)}, u32[]{:S(2)}, u32[]{:S(2)}) collective-permute-start(bf16[256,1024]{0,1:T(8,128)(2,1)} %copy.20), channel_id=1, source_target_pairs={{0,1},{1,2},{2,3},{3,4},{4,5},{5,6},{6,7},{7,8},{8,9},{9,10},{10,1... | collective-permute-start | bytes 1572872 | tf_op jit(solution)/shard_map/ppermute | solution.py:15
  12.0 11.6 %collective-permute-start.1 = (bf16[256,1024]{1,0:T(8,128)(2,1)}, bf16[256,1024]{1,0:T(8,128)(2,1)S(1)}, u32[]{:S(2)}, u32[]{:S(2)}) collective-permute-start(bf16[256,1024]{1,0:T(8,128)(2,1)} %collective-permute-done), channel_id=1, source_target_pairs={{0,1},{1,2},{2,3},{3,4},{4,5},{5,6},{6,7},{7,8},{8,9},{9,10},{10,1... | collective-permute-start | bytes 1572872 | tf_op jit(solution)/shard_map/ppermute | solution.py:15
  17.5 0.8 copy-start.4
  18.3 11.5 %collective-permute-start.5 = (bf16[256,1024]{0,1:T(8,128)(2,1)S(1)}, bf16[256,1024]{0,1:T(8,128)(2,1)}, u32[]{:S(2)}, u32[]{:S(2)}) collective-permute-start(bf16[256,1024]{0,1:T(8,128)(2,1)S(1)} %collective-permute-done.4), channel_id=1, source_target_pairs={{0,1},{1,2},{2,3},{3,4},{4,5},{5,6},{6,7},{7,8},{8,9},{9,10},{10,1... | collective-permute-start | bytes 1572872 | tf_op jit(solution)/shard_map/ppermute | solution.py:15
  23.6 6.2 %copy-start.6 = (bf16[256,1024]{1,0:T(8,128)(2,1)}, bf16[256,1024]{1,0:T(8,128)(2,1)S(1)}, u32[]{:S(2)}) copy-start(bf16[256,1024]{1,0:T(8,128)(2,1)S(1)} %collective-permute-done.1) | copy-start | bytes 1572868
  23.6 11.8 %collective-permute-start.2 = (bf16[256,1024]{1,0:T(8,128)(2,1)S(1)}, bf16[256,1024]{1,0:T(8,128)(2,1)}, u32[]{:S(2)}, u32[]{:S(2)}) collective-permute-start(bf16[256,1024]{1,0:T(8,128)(2,1)S(1)} %collective-permute-done.1), channel_id=1, source_target_pairs={{0,1},{1,2},{2,3},{3,4},{4,5},{5,6},{6,7},{7,8},{8,9},{9,10},{10,1... | collective-permute-start | bytes 1572872 | tf_op jit(solution)/shard_map/ppermute | solution.py:15
  29.8 11.7 %collective-permute-start.6 = (bf16[256,1024]{0,1:T(8,128)(2,1)}, bf16[256,1024]{0,1:T(8,128)(2,1)}, u32[]{:S(2)}, u32[]{:S(2)}) collective-permute-start(bf16[256,1024]{0,1:T(8,128)(2,1)} %collective-permute-done.5), channel_id=1, source_target_pairs={{0,1},{1,2},{2,3},{3,4},{4,5},{5,6},{6,7},{7,8},{8,9},{9,10},{10,1... | collective-permute-start | bytes 1572872 | tf_op jit(solution)/shard_map/ppermute | solution.py:15
  35.4 11.7 %collective-permute-start.3 = (bf16[256,1024]{1,0:T(8,128)(2,1)}, bf16[256,1024]{1,0:T(8,128)(2,1)}, u32[]{:S(2)}, u32[]{:S(2)}) collective-permute-start(bf16[256,1024]{1,0:T(8,128)(2,1)} %collective-permute-done.2), channel_id=1, source_target_pairs={{0,1},{1,2},{2,3},{3,4},{4,5},{5,6},{6,7},{7,8},{8,9},{9,10},{10,1... | collective-permute-start | bytes 1572872 | tf_op jit(solution)/shard_map/ppermute | solution.py:15
  39.9 11.5 %copy-start.3 = (bf16[256,1024]{1,0:T(8,128)(2,1)S(1)}, bf16[256,1024]{1,0:T(8,128)(2,1)}, u32[]{:S(2)}) copy-start(bf16[256,1024]{1,0:T(8,128)(2,1)} %param.8) | copy-start | bytes 1572868
  39.9 11.6 %copy-start.1 = (bf16[256,3072]{0,1:T(8,128)(2,1)S(1)}, bf16[256,3072]{0,1:T(8,128)(2,1)}, u32[]{:S(2)}) copy-start(bf16[256,3072]{0,1:T(8,128)(2,1)} %copy.18) | copy-start | bytes 4718596
  41.5 16.0 %collective-permute-start.7 = (bf16[256,1024]{0,1:T(8,128)(2,1)}, bf16[256,1024]{0,1:T(8,128)(2,1)S(1)}, u32[]{:S(2)}, u32[]{:S(2)}) collective-permute-start(bf16[256,1024]{0,1:T(8,128)(2,1)} %collective-permute-done.6), channel_id=1, source_target_pairs={{0,1},{1,2},{2,3},{3,4},{4,5},{5,6},{6,7},{7,8},{8,9},{9,10},{10,1... | collective-permute-start | bytes 1572872 | tf_op jit(solution)/shard_map/ppermute | solution.py:15
  56.7 3.0 %copy-start.5 = (bf16[256,1024]{0,1:T(8,128)(2,1)S(1)}, bf16[256,1024]{0,1:T(8,128)(2,1)}, u32[]{:S(2)}) copy-start(bf16[256,1024]{0,1:T(8,128)(2,1)} %copy-done.4) | copy-start | bytes 1572868
  56.7 3.0 %copy-start.2 = (bf16[256,1024]{0,1:T(8,128)(2,1)S(1)}, bf16[256,1024]{0,1:T(8,128)(2,1)}, u32[]{:S(2)}) copy-start(bf16[256,1024]{0,1:T(8,128)(2,1)} %copy.20) | copy-start | bytes 1572868
  69.8 1.4 %copy-start.8 = (bf16[3072,256]{1,0:T(8,128)(2,1)S(1)}, bf16[3072,256]{1,0:T(8,128)(2,1)}, u32[]{:S(2)}) copy-start(bf16[3072,256]{1,0:T(8,128)(2,1)} %param.11) | copy-start | bytes 4718596
  71.9 6.5 %collective-permute-start.8 = (bf16[2,8,8,256]{3,2,1,0:T(8,128)(2,1)S(1)}, bf16[2,8,8,256]{3,2,1,0:T(8,128)(2,1)S(1)}, u32[]{:S(2)}, u32[]{:S(2)}) collective-permute-start(bf16[2,8,8,256]{3,2,1,0:T(8,128)(2,1)S(1)} %bitcast.444), channel_id=1, source_target_pairs={{0,1},{1,2},{2,3},{3,4},{4,5},{5,6},{6,7},{7,8},{8,9},{9,10},{10,1... | collective-permute-start | bytes 196616 | tf_op jit(solution)/shard_map/ppermute | solution.py:15
  80.5 6.5 %collective-permute-start.9 = (bf16[2,8,8,256]{3,2,1,0:T(8,128)(2,1)S(1)}, bf16[2,8,8,256]{3,2,1,0:T(8,128)(2,1)S(1)}, u32[]{:S(2)}, u32[]{:S(2)}) collective-permute-start(bf16[2,8,8,256]{3,2,1,0:T(8,128)(2,1)S(1)} %bitcast.445), channel_id=1, source_target_pairs={{0,1},{1,2},{2,3},{3,4},{4,5},{5,6},{6,7},{7,8},{8,9},{9,10},{10,1... | collective-permute-start | bytes 196616 | tf_op jit(solution)/shard_map/ppermute | solution.py:15
  87.5 2.0 %copy-start.7 = (bf16[3,3,3,256,256]{4,3,2,1,0:T(8,128)(2,1)S(1)}, bf16[3,3,3,256,256]{4,3,2,1,0:T(8,128)(2,1)}, u32[]{:S(2)}) copy-start(bf16[3,3,3,256,256]{4,3,2,1,0:T(8,128)(2,1)} %param.13) | copy-start | bytes 10616836
where the time goes:
time: 91.9 us; the launch traced here: 91.2 us
  waiting for transfers between devices  32.7 us (36%)
  starting transfers between devices  21 us (23%)
  matrix products  15.7 us (17%)
  local copies, waits for them, and re-layouts  15.6 us (17%)
  other arithmetic  4.54 us (5%)
  between operations  1.7 us (2%)
    ppermute x10, waiting for transfers between devices, passed_along(): return lax.ppermute(block, axis, route)  32.7 us
    ppermute x10, starting transfers between devices, passed_along(): return lax.ppermute(block, axis, route)  21 us
    unnamed x87, local copies, waits for them, and re-layouts  14.6 us
    dot_general x8, matrix products, attend(): jnp.einsum('rts,sd->rtd', probs, vpart, preferred_element_type=jnp.float32)  6.3 us
    dot_general x8, matrix products, attend(): jnp.einsum('trd,sd->rts', qpart, kpart, preferred_element_type=jnp.float32)  5.92 us
    reduce_sum x8, other arithmetic, attend(): total = jnp.sum(weights, axis=-1)  4.45 us
    dot_general x2, matrix products, conv_valid(): jnp.dot(columns, weight.reshape(27 * chans, weight.shape[4]), preferred_e...  2.85 us
  transfers between devices with their start and end apart: 10, of which 9 were waited for; matrix products, arithmetic and copies ran while one was open for 16% of the time, Pallas kernels for 0%

commit v1 on v0

v1 whole, which is shorter than its diff:
```python
import functools

import jax
import jax.numpy as jnp
from jax import lax
from jax.experimental import pallas as pl
from jax.experimental.pallas import tpu as pltpu
from jax.sharding import PartitionSpec as P

HEAD_DIM = 128
FRAMES = 4
ROWS = 8
COLS = 8
REACH = 4
LOG2E = 1.4426950408889634
MESH = pl.DeviceIdType.MESH
DOT_T = (((1,), (1,)), ((), ()))


def kernel(n, q_hbm, k_hbm, v_hbm, look, w_hbm, c1_hbm, c2_hbm, out,
           q, kv, w, c1, c2, acc, halo_out, halo_in, ext,
           kv_sem, q_sem, w_sem, send, recv, halo_send, halo_recv):
    me = lax.axis_index("span")
    core = lax.rem(me, 2)
    side = lax.rem(me // 2, 2)
    groups = kv.shape[1]
    tok = q.shape[1]
    chans = acc.shape[1]
    wide = q.shape[2]
    ratio = wide // HEAD_DIM
    area = ROWS * COLS
    partner = me + 1 - 2 * core
    across = me + 2 - 4 * side

    def local_kv(g, half):
        src = (k_hbm, v_hbm)[half]
        cols = pl.ds(g * HEAD_DIM, HEAD_DIM)
        return pltpu.make_async_copy(src.at[:, cols], kv.at[0, g, half], kv_sem.at[g, half])

    def local_q(g):
        start = g * wide if isinstance(g, int) else pl.multiple_of(g * wide, wide)
        return pltpu.make_async_copy(q_hbm.at[:, pl.ds(start, wide)], q.at[g], q_sem.at[g])

    weights = [
        pltpu.make_async_copy(src, dst, w_sem.at[i])
        for i, (src, dst) in enumerate(((w_hbm, w), (c1_hbm, c1), (c2_hbm, c2)))
    ]

    def remote(src_slot, dst_slot, g, lane, target):
        return pltpu.make_async_remote_copy(
            src_ref=kv.at[src_slot, g],
            dst_ref=kv.at[dst_slot, g],
            send_sem=send.at[lane, g],
            recv_sem=recv.at[dst_slot, g],
            device_id={"span": target},
            device_id_type=MESH,
        )

    def arrived(slot, g):
        remote(slot, slot, g, 0, partner).wait_recv()

    for g in range(groups):
        for half in range(2):
            local_kv(g, half).start()
    for g in range(groups):
        local_q(g).start()
    for copy in weights:
        copy.start()

    barrier = pltpu.get_barrier_semaphore()
    near = (
        (me >= 4, me - 4),
        (me + 4 < n, me + 4),
        (me >= 1, me - 1),
        (me + 1 < n, me + 1),
        (me >= 0, across),
    )
    for there, target in near:
        @pl.when(there)
        def _():
            pl.semaphore_signal(barrier, inc=1, device_id={"span": target}, device_id_type=MESH)
    count = sum(jnp.where(there, 1, 0).astype(jnp.int32) for there, _unused in near)
    pl.semaphore_wait(barrier, count)

    @pl.loop(0, groups)
    def _(g):
        for half in range(2):
            pltpu.make_async_copy(
                k_hbm.at[:, pl.ds(0, HEAD_DIM)], kv.at[0, g, half], kv_sem.at[g, half]
            ).wait()

        @pl.when(me + 4 < n)
        def _():
            remote(0, 4, g, 0, me + 4).start()

        @pl.when(side == 0)
        def _():
            remote(0, 2, g, 1, across).start()

        @pl.when(core == 0)
        def _():
            remote(0, 1, g, 2, partner).start()

    for slot in range(1, REACH + 1):
        @pl.when(me < slot)
        def _():
            kv[slot] = jnp.zeros(kv.shape[1:], kv.dtype)

    weights[0].wait()
    acc[...] = jnp.zeros_like(acc)
    bias = [jnp.where(j <= look[0], 0.0, 1e30).astype(jnp.float32) for j in range(REACH + 1)]
    factor = LOG2E / HEAD_DIM**0.5
    ones = jnp.ones((tok, HEAD_DIM), jnp.bfloat16)

    def attend(g):
        heads = []
        for r in range(ratio):
            query = q[g, :, r * HEAD_DIM : (r + 1) * HEAD_DIM]
            scores = []
            top = None
            for j in range(REACH + 1):
                s = lax.dot_general(query, kv[j, g, 0], DOT_T, preferred_element_type=jnp.float32)
                scores.append(s)
                peak = s[:, :HEAD_DIM]
                for start in range(HEAD_DIM, tok, HEAD_DIM):
                    peak = jnp.maximum(peak, s[:, start : start + HEAD_DIM])
                peak = peak - bias[j]
                top = peak if top is None else jnp.maximum(top, peak)
            top = jnp.max(top, axis=1, keepdims=True)
            mixed = None
            for j in range(REACH + 1):
                probs = jnp.exp2((scores[j] - (top + bias[j])) * factor).astype(jnp.bfloat16)
                vals = jnp.concatenate([kv[j, g, 1], ones], axis=1)
                part = jnp.dot(probs, vals, preferred_element_type=jnp.float32)
                mixed = part if mixed is None else mixed + part
            heads.append((mixed[:, :HEAD_DIM] / mixed[:, HEAD_DIM:]).astype(jnp.bfloat16))
        attended = jnp.concatenate(heads, axis=1)
        rows = pl.ds(pl.multiple_of(g * wide, wide), wide)
        acc[...] += jnp.dot(attended, w[rows, :], preferred_element_type=jnp.float32)

    @pl.loop(0, groups + 2)
    def _(t):
        @pl.when((t < groups) & (me >= 4))
        def _():
            arrived(4, t)

            @pl.when(side == 1)
            def _():
                remote(4, 2, t, 1, across).start()

            @pl.when(core == 1)
            def _():
                remote(4, 3, t, 2, partner).start()

        @pl.when((t >= 1) & (t <= groups) & (me >= 2))
        def _():
            arrived(2, t - 1)

            @pl.when(core == 0)
            def _():
                remote(2, 3, t - 1, 3, partner).start()

            @pl.when(core == 1)
            def _():
                remote(2, 1, t - 1, 3, partner).start()

        @pl.when(t >= 2)
        def _():
            g = t - 2

            @pl.when(me >= 1)
            def _():
                arrived(1, g)

            @pl.when(me >= 3)
            def _():
                arrived(3, g)

            local_q(g).wait()
            attend(g)

    frame = lax.broadcasted_iota(jnp.int32, (2 * area, chans), 0)
    column = lax.rem(frame, COLS)

    def halo(which):
        return pltpu.make_async_remote_copy(
            src_ref=halo_out.at[which],
            dst_ref=halo_in.at[which],
            send_sem=halo_send.at[which],
            recv_sem=halo_recv.at[which],
            device_id={"span": lax.rem(me + 1, n)},
            device_id_type=MESH,
        )

    def place(layer, first, x):
        shifted = (
            jnp.where(column == 0, 0.0, pltpu.roll(x, 1, 0)),
            x,
            jnp.where(column == COLS - 1, 0.0, pltpu.roll(x, 2 * area - 1, 0)),
        )
        for e in range(3):
            for f in range(2):
                ext[layer, e, first + f, COLS : COLS + area, :] = shifted[e][f * area : (f + 1) * area]

    def conv(layer, weight, first):
        total = None
        for a in range(3):
            taps = []
            for b in range(3):
                for e in range(3):
                    taps.append(jnp.concatenate(
                        [
                            ext[layer, e, first + f + a, b * COLS : b * COLS + area, :]
                            for f in range(2)
                        ], axis=0).astype(jnp.bfloat16))
            part = jnp.dot(
                jnp.concatenate(taps, axis=1),
                weight[a * 9 * chans : (a + 1) * 9 * chans, :],
                preferred_element_type=jnp.float32,
            )
            total = part if total is None else total + part
        return total

    edge = jnp.zeros((2, 3, FRAMES + 2, COLS, chans), jnp.float32)
    ext[:, :, :, :COLS, :] = edge
    ext[:, :, :, COLS + area :, :] = edge

    def send_halo(which, x):
        halo_out[which] = x

        @pl.when(me + 1 < n)
        def _():
            halo(which).start()

    def receive_halo(which):
        @pl.when(me == 0)
        def _():
            halo_in[which] = jnp.zeros(halo_in.shape[1:], halo_in.dtype)

        @pl.when(me >= 1)
        def _():
            halo(which).wait_recv()

        place(which, 0, halo_in[which].astype(jnp.float32))

    half = 2 * area
    latent = acc[half:, :].astype(jnp.bfloat16)
    send_halo(0, latent)
    place(0, 4, latent.astype(jnp.float32))
    place(0, 2, acc[:half, :].astype(jnp.bfloat16).astype(jnp.float32))
    weights[1].wait()
    hidden = jax.nn.silu(conv(0, c1, 2)).astype(jnp.bfloat16)
    send_halo(1, hidden)
    place(1, 4, hidden.astype(jnp.float32))
    receive_halo(0)
    hidden = jax.nn.silu(conv(0, c1, 0)).astype(jnp.bfloat16)
    place(1, 2, hidden.astype(jnp.float32))
    weights[2].wait()
    out[half:, :] = conv(1, c2, 2).astype(out.dtype)
    receive_halo(1)
    out[:half, :] = conv(1, c2, 0).astype(out.dtype)

    @pl.when(me + 1 < n)
    def _():
        for which in range(2):
            halo(which).wait_send()

    @pl.loop(0, groups)
    def _(g):
        @pl.when(me + 4 < n)
        def _():
            remote(0, 4, g, 0, partner).wait_send()

        @pl.when((side == 0) | (me >= 4))
        def _():
            remote(0, 2, g, 1, partner).wait_send()

        @pl.when((core == 0) | (me >= 4))
        def _():
            remote(0, 1, g, 2, partner).wait_send()

        @pl.when(me >= 2)
        def _():
            remote(2, 3, g, 3, partner).wait_send()


def on_device(n, queries, keys, values, lookback, w_out, conv_first, conv_second):
    tok = queries.shape[0]
    chans = w_out.shape[1]
    groups = keys.shape[1] // HEAD_DIM
    wide = queries.shape[1] // groups
    taps = 27 * chans
    area = ROWS * COLS
    hbm = pl.BlockSpec(memory_space=pltpu.HBM)
    bf16 = jnp.bfloat16
    dma = pltpu.SemaphoreType.DMA
    return pl.pallas_call(
        functools.partial(kernel, n),
        out_shape=jax.ShapeDtypeStruct((tok, chans), bf16),
        in_specs=[hbm, hbm, hbm, pl.BlockSpec(memory_space=pltpu.SMEM), hbm, hbm, hbm],
        out_specs=pl.BlockSpec(memory_space=pltpu.VMEM),
        scratch_shapes=[
            pltpu.VMEM((groups, tok, wide), bf16),
            pltpu.VMEM((REACH + 1, groups, 2, tok, HEAD_DIM), bf16),
            pltpu.VMEM(w_out.shape, bf16),
            pltpu.VMEM((taps, chans), bf16),
            pltpu.VMEM((taps, chans), bf16),
            pltpu.VMEM((tok, chans), jnp.float32),
            pltpu.VMEM((2, 2 * area, chans), bf16),
            pltpu.VMEM((2, 2 * area, chans), bf16),
            pltpu.VMEM((2, 3, FRAMES + 2, area + 2 * COLS, chans), jnp.float32),
            dma((groups, 2)),
            dma((groups,)),
            dma((3,)),
            dma((4, groups)),
            dma((REACH + 1, groups)),
            dma((2,)),
            dma((2,)),
        ],
        compiler_params=pltpu.CompilerParams(
            collective_id=0, has_side_effects=True, vmem_limit_bytes=56 * 1024 * 1024
        ),
    )(
        queries, keys, values, lookback, w_out,
        conv_first.reshape(taps, chans), conv_second.reshape(taps, chans),
    )


def solution(mesh):
    placed = (
        P(("groups", "span"), None),
        P(("groups", "span"), None),
        P(("groups", "span"), None),
        P(("groups", "span")),
        P(),
        P(),
        P(),
    )
    return jax.shard_map(
        functools.partial(on_device, mesh.shape["span"]),
        mesh=mesh,
        in_specs=placed,
        out_specs=P(("groups", "span"), None),
        check_vma=False,
    )
```

time: 91.9 us -> 43.2 us (0.47)
  Pallas kernels: 0 us -> 40.5 us
  waiting for transfers between devices: 32.7 us -> 0 us
  starting transfers between devices: 21 us -> 0 us
  matrix products: 15.7 us -> 0 us
  local copies, waits for them, and re-layouts: 15.6 us -> 1.57 us
  other arithmetic: 4.54 us -> 0 us
  between operations: 1.7 us -> 0.66 us
    pallas_call x0 -> x1, Pallas kernels: none -> 40.5 us  [on_device(): pl.pallas_call(functools.partial(kernel, n), out_shape=jax.ShapeDtypeStru...]
    ppermute x10 -> x0, waiting for transfers between devices: 32.7 us -> none  [passed_along(): return lax.ppermute(block, axis, route)]
    ppermute x10 -> x0, starting transfers between devices: 21 us -> none  [passed_along(): return lax.ppermute(block, axis, route)]
    dot_general x19 -> x0, matrix products: 15.7 us -> none  [the longest x8 6.3 us: attend(): jnp.einsum('rts,sd->rtd', probs, vpart, preferred_element_type=jnp.float32)]
    unnamed x87 -> x1, local copies, waits for them, and re-layouts: 14.6 us -> 1.57 us
    reduce_sum x8 -> x0, other arithmetic: 4.45 us -> none  [attend(): total = jnp.sum(weights, axis=-1)]
  transfers between devices with their start and end apart: 10 -> 0, of which waited for: 9 -> 0; matrix products, arithmetic and copies ran while one was open for 16% -> 0% of each run, Pallas kernels for 0% -> 0%
where the time goes in v1:
time: 43.2 us; the launch traced here: 42.7 us
  Pallas kernels  40.5 us (94%)
  local copies, waits for them, and re-layouts  1.57 us (4%)
  between operations  0.66 us (2%)
    pallas_call x1, Pallas kernels, on_device(): pl.pallas_call(functools.partial(kernel, n), out_shape=jax.ShapeDtypeStru...  40.5 us
    unnamed x1, local copies, waits for them, and re-layouts  1.57 us

profile of v1, /device:TPU:12, one launch (start us, length us, event | category | flops | bytes accessed | tf_op | source)
XLA Modules:
  0.0 42.7 jit_solution(13287796256148310186)
XLA Ops:
  0.7 40.5 %shard_map.73 = bf16[256,256]{1,0:T(8,128)(2,1)} custom-call(bf16[256,3072]{1,0:T(8,128)(2,1)} %q_hbm.1, bf16[256,1024]{1,0:T(8,128)(2,1)} %k_hbm.1, bf16[256,1024]{1,0:T(8,128)(2,1)} %v_hbm.1, s32[1]{0:T(128)S(6)} %copy.9.look, bf16[3072,256]{1,0:T(8,128)(2,1)} %w_hbm.1, bf16[6912,256]{1,0:T(8,128)(2,1)} %bitcast.2, bf16[6912,256]{1,0:T(8,128)(2,1)} %bitcast.3), custom_call_target="tpu_custom_call" | custom-call | tf_op jit(solution)/shard_map/pallas_call | solution.py:297
  41.2 1.6 %copy.10 = bf16[256,256]{1,0:T(8,128)(2,1)} copy(bf16[256,256]{1,0:T(8,128)(2,1)} %shard_map.73) | data formatting | bytes 262144

commit v2 on v1

--- a/solution.py
+++ b/solution.py
@@ -296,7 +296,7 @@
     dma = pltpu.SemaphoreType.DMA
     return pl.pallas_call(
         functools.partial(kernel, n),
-        out_shape=jax.ShapeDtypeStruct((tok, chans), bf16),
+        out_shape=pltpu.VMEM((tok, chans), bf16),
         in_specs=[hbm, hbm, hbm, pl.BlockSpec(memory_space=pltpu.SMEM), hbm, hbm, hbm],
         out_specs=pl.BlockSpec(memory_space=pltpu.VMEM),
         scratch_shapes=[

time: 43.2 us -> 41.6 us (0.963)
  local copies, waits for them, and re-layouts: 1.57 us -> 0.66 us
  Pallas kernels: 40.5 us -> 39.9 us
    unnamed x1, local copies, waits for them, and re-layouts: 1.57 us -> 0.66 us
    pallas_call x1, Pallas kernels: 40.5 us -> 39.9 us  [on_device(): pl.pallas_call(functools.partial(kernel, n), out_shape=pltpu.VMEM((tok, c...]
where the time goes in v2:
time: 41.6 us; the launch traced here: 41.2 us
  Pallas kernels  39.9 us (96%)
  local copies, waits for them, and re-layouts  0.66 us (2%)
  between operations  0.66 us (2%)
    pallas_call x1, Pallas kernels, on_device(): pl.pallas_call(functools.partial(kernel, n), out_shape=pltpu.VMEM((tok, c...  39.9 us

profile of v2, /device:TPU:12, one launch (start us, length us, event | category | flops | bytes accessed | tf_op | source)
XLA Modules:
  0.0 41.2 jit_solution(6074604013533025296)
XLA Ops:
  0.7 39.9 %shard_map.73 = bf16[256,256]{1,0:T(8,128)(2,1)S(1)} custom-call(bf16[256,3072]{1,0:T(8,128)(2,1)} %q_hbm.1, bf16[256,1024]{1,0:T(8,128)(2,1)} %k_hbm.1, bf16[256,1024]{1,0:T(8,128)(2,1)} %v_hbm.1, s32[1]{0:T(128)S(6)} %copy.10.look, bf16[3072,256]{1,0:T(8,128)(2,1)} %w_hbm.1, bf16[6912,256]{1,0:T(8,128)(2,1)} %bitcast.2, bf16[6912,256]{1,0:T(8,128)(2,1)} %bitcast.3), custom_call_target="tpu_custom_call" | custom-call | tf_op jit(solution)/shard_map/pallas_call | solution.py:297
  40.5 0.7 %copy.9 = bf16[256,256]{1,0:T(8,128)(2,1)} copy(bf16[256,256]{1,0:T(8,128)(2,1)S(1)} %shard_map.73) | data formatting | bytes 262144
